TPU v7x, 256 devices: a whole 4x4x8 slice. The times are simulated.
256 devices in a mesh: gx: 8 (over y, core), gy: 32 (over z, x).
Axes of the slice: x: 4, y: 4, z: 8, core: 2. Of those that a mesh axis runs over, the one named last changes fastest.
Arguments:
- dual_operators: float32 [16, 32, 1024, 1024], P('gx', 'gy')
- rigid_trace: float32 [16, 32, 6, 1024], P('gx', 'gy'), may hold values from -0.1875 to 0.1875
- coarse_inverse: float32 [8, 32, 12, 3072], P('gx', 'gy'), as said below
- floating: int32 [16, 32], P('gx', 'gy'), may hold values 0 or 1
- block_map: int32 [16, 32, 8], P('gx', 'gy'), may hold values from 0 to 7, each once within a row
- interface_gap: float32 [16, 32, 32, 1024], P('gx', 'gy'), may hold values from -6 to 6
- rigid_load: float32 [16, 32, 6, 32], P('gx', 'gy'), may hold values from -24 to 24
Outputs:
- dual_solution: float32 [16, 32, 32, 1024], P('gx', 'gy')
- dual_residual: float32 [16, 32, 32, 1024], P('gx', 'gy')
Inputs may be any that keep to these rules, and one draw needn't show every extreme that they name: coarse_inverse read as a square matrix is exactly symmetric.
All inputs are finite; a program needn't handle non-finite values. No bound on the sum of `floating` on one device may be relied on, other than what follows from the above.
Results may differ from a plain program's by a relative error of at most 0.0003.
Values sent between devices are 32-bit elements; how exact they have to be, the bound alone decides.
No kernel may reach another device: no remote copies, remote signals or barrier semaphores. Data moves between devices by JAX's collectives and lax.ppermute only.
A program may use at most 64 MiB of HBM per device.

v0:
```python
import jax
import jax.numpy as jnp
from jax import lax
from jax.sharding import PartitionSpec as P

ITERS = 2


HI = lax.Precision.HIGHEST


def shifted(value, axis, steps):
    count = lax.axis_size(axis)
    initial, last = (max(0, -steps), min(count, count - steps))
    return lax.ppermute(value, axis, [(source, source + steps) for source in range(initial, last)])


def slot_table(block_map):
    slots = jnp.arange(8, dtype=jnp.int32)
    return (block_map[..., None, :] == slots[:, None]).astype(jnp.float32)


def slot_weights(first, second, sx_all, sy_all):
    first_b, second_b = jnp.broadcast_arrays(first, second)
    outside = jnp.stack(
        [first_b == 0, first_b == sx_all - 1, second_b == 0, second_b == sy_all - 1], -1
    )
    outside = jnp.repeat(outside, 2, axis=-1)
    return jnp.where(outside, 1.0, 0.5).astype(jnp.float32)


def chol_solve(matrix, right):
    lower = jnp.linalg.cholesky(matrix)
    middle = lax.linalg.triangular_solve(lower, right, left_side=True, lower=True)
    return lax.linalg.triangular_solve(lower, middle, left_side=True, lower=True, transpose_a=True)


def per_device(
    dual_operators, rigid_trace, coarse_inverse, floating, block_map, interface_gap, rigid_load
):
    count_x = lax.axis_size("gx")
    count_y = lax.axis_size("gy")
    place_x = lax.axis_index("gx")
    place_y = lax.axis_index("gy")
    table = slot_table(block_map)
    first = 2 * place_x + jnp.arange(2, dtype=jnp.int32)[:, None]
    second = jnp.full((1, 1), place_y, jnp.int32)
    omega = slot_weights(first, second, 2 * count_x, count_y)
    wblock = jnp.einsum("abqk,abq->abk", table, omega, precision=HI)
    wloc = jnp.repeat(wblock, rigid_trace.shape[3] // 8, axis=-1)
    live = floating.astype(jnp.float32)[:, :, None, None]
    rows_local = coarse_inverse.reshape(coarse_inverse.shape[2], coarse_inverse.shape[3])

    def jump(field):
        subs, cols, width_cases, width = field.shape
        blocks = field.reshape(subs, cols, width_cases, 8, width // 8)
        slot = jnp.einsum("abqk,abrkc->abrqc", table, blocks, precision=HI)
        from_below = shifted(slot[1:2, :, :, 2:4], "gx", 1)
        from_above = shifted(slot[0:1, :, :, 0:2], "gx", -1)
        lower_y = shifted(slot[:, :, :, 6:8], "gy", 1)
        upper_y = shifted(slot[:, :, :, 4:6], "gy", -1)
        lower_x = jnp.concatenate([from_below, slot[0:1, :, :, 2:4]], 0)
        upper_x = jnp.concatenate([slot[1:2, :, :, 0:2], from_above], 0)
        partner = jnp.concatenate([lower_x, upper_x, lower_y, upper_y], 3)
        back = jnp.einsum("abqk,abrqc->abrkc", table, slot - partner, precision=HI)
        return back.reshape(subs, cols, width_cases, width)

    def inner(left, right):
        return jnp.einsum("abrk,absk->rs", left * wloc[:, :, None, :], right, precision=HI)

    def modes(load):
        mine = load.reshape(-1, load.shape[-1])
        piece = lax.all_gather(mine, ("gx", "gy"), axis=0, tiled=True)
        piece_rows = lax.slice_in_dim(rows_local, 0, piece.shape[0], axis=1)
        alpha = jnp.zeros_like(mine) + jnp.dot(piece_rows, piece, precision=HI)
        return alpha.reshape(load.shape) * live

    def spread(alpha):
        return jump(jnp.einsum("abmr,abmk->abrk", alpha, rigid_trace, precision=HI))

    def project(field):
        load = jnp.einsum("abmk,abrk->abmr", rigid_trace, field, precision=HI) * live
        return field - spread(modes(load))

    def applied(field):
        return jnp.einsum("abrk,abkj->abrj", field, dual_operators, precision=HI)

    def combine(field, mixing):
        return jnp.einsum("abrk,rs->absk", field, mixing, precision=HI)

    solution = spread(modes(rigid_load * live))
    resid = project(jump(interface_gap - applied(solution)))
    direction = resid
    for step in range(ITERS):
        moved = project(direction)
        image = project(jump(applied(moved)))
        curvature, drive = lax.psum(
            (inner(direction, image), inner(direction, resid)), ("gx", "gy")
        )
        step_len = chol_solve(curvature, drive)
        solution = solution + combine(moved, step_len)
        resid = resid - combine(image, step_len)
        if step + 1 < ITERS:
            cross_new = lax.psum(inner(image, resid), ("gx", "gy"))
            coupling = chol_solve(curvature, cross_new)
            direction = resid - combine(direction, coupling)
    return (solution, resid)


def solution(mesh):
    return jax.shard_map(
        per_device,
        mesh=mesh,
        in_specs=(
            P("gx", "gy", None, None),
            P("gx", "gy", None, None),
            P("gx", "gy", None, None),
            P("gx", "gy"),
            P("gx", "gy", None),
            P("gx", "gy", None, None),
            P("gx", "gy", None, None),
        ),
        out_specs=(P("gx", "gy", None, None), P("gx", "gy", None, None)),
        check_vma=False,
    )
```

profile of v0, /device:TPU:1, one launch (start us, length us, event | category | flops | bytes accessed | tf_op | source)
XLA Modules:
  0.0 871.3 jit_solution(16072218619224499770)
XLA Ops:
  2.1 76.3 %all-gather = f32[256,12,32]{2,1,0:T(8,128)S(1)} all-gather(f32[1,12,32]{2,1,0:T(8,128)S(1)} %copy.103), channel_id=1, replica_groups=mesh['gx'=8,'gy'=32] {'gx','gy'}, dimensions={0}, use_global_device_ids=true | all-gather | bytes 394752 | tf_op jit(solution)/shard_map/all_gather | solution.py:73
  78.4 1.3 reshape.525
  79.7 2.4 convolution_bitcast_fusion.36
  83.2 1.4 collective-permute-start.2
  85.9 2.9 collective-permute-start
  88.8 3.9 collective-permute-start.1
  92.7 1.4 collective-permute-done.1
  94.5 7.2 fusion.16
  102.3 4.3 collective-permute-start.6
  107.9 2.2 collective-permute-start.4
  110.1 2.1 collective-permute-start.5
  112.3 3.1 collective-permute-done.5
  116.5 74.7 %all-gather.1 = f32[256,12,32]{2,1,0:T(8,128)S(1)} all-gather(f32[1,12,32]{2,1,0:T(8,128)S(1)} %reshape.526), channel_id=1, replica_groups=mesh['gx'=8,'gy'=32] {'gx','gy'}, dimensions={0}, use_global_device_ids=true | all-gather | bytes 394752 | tf_op jit(solution)/shard_map/all_gather | solution.py:73
  191.2 1.3 reshape.527
  192.5 2.4 convolution_bitcast_fusion.35
  195.9 1.9 collective-permute-start.10
  199.2 3.6 collective-permute-start.8
  202.8 2.6 collective-permute-start.9
  205.4 2.6 collective-permute-done.9
  209.1 73.9 %all-gather.2 = f32[256,12,32]{2,1,0:T(8,128)S(1)} all-gather(f32[1,12,32]{2,1,0:T(8,128)S(1)} %reshape.528), channel_id=1, replica_groups=mesh['gx'=8,'gy'=32] {'gx','gy'}, dimensions={0}, use_global_device_ids=true | all-gather | bytes 394752 | tf_op jit(solution)/shard_map/all_gather | solution.py:73
  283.0 1.3 reshape.529
  284.3 2.4 convolution_bitcast_fusion.34
  287.8 1.9 collective-permute-start.14
  291.0 3.6 collective-permute-start.12
  294.7 2.6 collective-permute-start.13
  297.5 2.5 collective-permute-done.13
  300.4 7.2 fusion.2
  308.1 4.3 collective-permute-start.18
  313.7 2.2 collective-permute-start.16
  315.9 2.1 collective-permute-start.17
  318.3 2.9 collective-permute-done.17
  321.9 76.7 %all-gather.3 = f32[256,12,32]{2,1,0:T(8,128)S(1)} all-gather(f32[1,12,32]{2,1,0:T(8,128)S(1)} %reshape.530), channel_id=1, replica_groups=mesh['gx'=8,'gy'=32] {'gx','gy'}, dimensions={0}, use_global_device_ids=true | all-gather | bytes 394752 | tf_op jit(solution)/shard_map/all_gather | solution.py:73
  398.7 1.3 reshape.531
  400.0 2.4 convolution_bitcast_fusion.33
  403.5 1.9 collective-permute-start.22
  406.7 3.6 collective-permute-start.20
  410.3 2.8 collective-permute-start.21
  413.3 2.3 collective-permute-done.21
  417.0 80.4 %all-reduce.1 = (f32[32,32]{1,0:T(8,128)S(1)}, f32[32,32]{0,1:T(8,128)S(1)}) all-reduce(f32[32,32]{1,0:T(8,128)S(1)} %convolution_bitcast_fusion.29, f32[32,32]{0,1:T(8,128)S(1)} %convolution_bitcast_fusion.30), channel_id=1, replica_groups=mesh['gx'=8,'gy'=32] {'gx','gy'}, use_global_device_ids=true, to_apply=%region_3.5 | all-reduce | flops 2048 | bytes 16384 | tf_op jit(solution)/shard_map/psum | solution.py:97
  497.5 2.9 cholesky.44
  501.7 2.4 custom-call.13
  505.4 74.3 %psum.37 = f32[32,32]{1,0:T(8,128)S(1)} all-reduce(f32[32,32]{1,0:T(8,128)S(1)} %convolution_bitcast_fusion.28), channel_id=1, replica_groups=mesh['gx'=8,'gy'=32] {'gx','gy'}, use_global_device_ids=true, to_apply=%region_4.8 | all-reduce | flops 1024 | bytes 8192 | tf_op jit(solution)/shard_map/psum | solution.py:104
  580.9 69.6 %all-gather.4 = f32[256,12,32]{2,1,0:T(8,128)S(1)} all-gather(f32[1,12,32]{2,1,0:T(8,128)S(1)} %reshape.532), channel_id=1, replica_groups=mesh['gx'=8,'gy'=32] {'gx','gy'}, dimensions={0}, use_global_device_ids=true | all-gather | bytes 394752 | tf_op jit(solution)/shard_map/all_gather | solution.py:73
  650.4 1.3 reshape.533
  651.7 2.4 convolution_bitcast_fusion.32
  655.1 1.8 collective-permute-start.26
  658.2 2.7 collective-permute-start.24
  661.0 3.7 collective-permute-start.25
  664.7 1.5 collective-permute-done.25
  666.7 7.2 fusion
  674.4 4.3 collective-permute-start.30
  680.0 2.2 collective-permute-start.28
  682.2 2.3 collective-permute-start.29
  685.4 2.0 collective-permute-done.29
  688.6 74.6 %all-gather.5 = f32[256,12,32]{2,1,0:T(8,128)S(1)} all-gather(f32[1,12,32]{2,1,0:T(8,128)S(1)} %reshape.534), channel_id=1, replica_groups=mesh['gx'=8,'gy'=32] {'gx','gy'}, dimensions={0}, use_global_device_ids=true | all-gather | bytes 394752 | tf_op jit(solution)/shard_map/all_gather | solution.py:73
  763.3 1.3 reshape.535
  764.6 2.4 convolution_bitcast_fusion.31
  768.0 1.7 collective-permute-start.34
  771.0 3.7 collective-permute-start.32
  774.7 2.8 collective-permute-start.33
  777.9 2.1 collective-permute-done.33
  780.8 80.5 %all-reduce = (f32[32,32]{1,0:T(8,128)S(1)}, f32[32,32]{0,1:T(8,128)S(1)}) all-reduce(f32[32,32]{1,0:T(8,128)S(1)} %convolution_bitcast_fusion.26, f32[32,32]{0,1:T(8,128)S(1)} %convolution_bitcast_fusion.27), channel_id=1, replica_groups=mesh['gx'=8,'gy'=32] {'gx','gy'}, use_global_device_ids=true, to_apply=%region_6.10 | all-reduce | flops 2048 | bytes 16384 | tf_op jit(solution)/shard_map/psum | solution.py:97
  861.4 2.9 cholesky.55
  865.7 2.4 custom-call.17
  (192 shorter events, 38.2 us)
Async XLA Ops:
  78.4 1.3 copy-start
  79.7 2.4 copy-start.16
  79.7 3.0 copy-start.15
  82.1 12.4 %copy-start.14 = (f32[2,1,32,1024]{3,2,1,0:T(8,128)S(1)}, f32[2,1,32,1024]{3,2,1,0:T(8,128)}, u32[]{:S(2)}) copy-start(f32[2,1,32,1024]{3,2,1,0:T(8,128)} %param.17) | copy-start | bytes 786436
  83.2 10.9 %collective-permute-start.2 = (f32[2,1,32,2,128]{4,3,2,0,1:T(2,128)S(1)}, f32[2,1,32,2,128]{4,3,2,0,1:T(2,128)S(1)}, u32[]{:S(2)}, u32[]{:S(2)}) collective-permute-start(f32[2,1,32,2,128]{4,3,2,0,1:T(2,128)S(1)} %get-tuple-element.73), channel_id=1, source_target_pairs={{0,1},{1,2},{2,3},{3,4},{4,5},{5,6},{6,7},{7,8},{8,9},{9,10},{10,1... | collective-permute-start | bytes 196616 | tf_op jit(solution)/shard_map/ppermute | solution.py:15
  84.6 9.5 %collective-permute-start.3 = (f32[2,1,32,2,128]{4,3,2,0,1:T(2,128)S(1)}, f32[2,1,32,2,128]{4,3,2,0,1:T(2,128)S(1)}, u32[]{:S(2)}, u32[]{:S(2)}) collective-permute-start(f32[2,1,32,2,128]{4,3,2,0,1:T(2,128)S(1)} %get-tuple-element.74), channel_id=1, source_target_pairs={{1,0},{2,1},{3,2},{4,3},{5,4},{6,5},{7,6},{8,7},{9,8},{10,9},{11,1... | collective-permute-start | bytes 196616 | tf_op jit(solution)/shard_map/ppermute | solution.py:15
  85.9 6.8 collective-permute-start
  88.8 5.2 collective-permute-start.1
  94.5 7.3 copy-start.3
  102.3 13.1 %collective-permute-start.6 = (f32[2,1,32,2,128]{4,3,2,0,1:T(2,128)S(1)}, f32[2,1,32,2,128]{4,3,2,0,1:T(2,128)S(1)}, u32[]{:S(2)}, u32[]{:S(2)}) collective-permute-start(f32[2,1,32,2,128]{4,3,2,0,1:T(2,128)S(1)} %get-tuple-element.67), channel_id=1, source_target_pairs={{0,1},{1,2},{2,3},{3,4},{4,5},{5,6},{6,7},{7,8},{8,9},{9,10},{10,1... | collective-permute-start | bytes 196616 | tf_op jit(solution)/shard_map/ppermute | solution.py:15
  106.6 8.8 %collective-permute-start.7 = (f32[2,1,32,2,128]{4,3,2,0,1:T(2,128)S(1)}, f32[2,1,32,2,128]{4,3,2,0,1:T(2,128)S(1)}, u32[]{:S(2)}, u32[]{:S(2)}) collective-permute-start(f32[2,1,32,2,128]{4,3,2,0,1:T(2,128)S(1)} %get-tuple-element.68), channel_id=1, source_target_pairs={{1,0},{2,1},{3,2},{4,3},{5,4},{6,5},{7,6},{8,7},{9,8},{10,9},{11,1... | collective-permute-start | bytes 196616 | tf_op jit(solution)/shard_map/ppermute | solution.py:15
  107.9 4.3 collective-permute-start.4
  110.1 5.2 collective-permute-start.5
  115.8 0.7 copy-start.8
  195.9 12.1 %collective-permute-start.10 = (f32[2,1,32,2,128]{4,3,2,0,1:T(2,128)S(1)}, f32[2,1,32,2,128]{4,3,2,0,1:T(2,128)S(1)}, u32[]{:S(2)}, u32[]{:S(2)}) collective-permute-start(f32[2,1,32,2,128]{4,3,2,0,1:T(2,128)S(1)} %get-tuple-element.61), channel_id=1, source_target_pairs={{0,1},{1,2},{2,3},{3,4},{4,5},{5,6},{6,7},{7,8},{8,9},{9,10},{10,1... | collective-permute-start | bytes 196616 | tf_op jit(solution)/shard_map/ppermute | solution.py:15
  197.9 10.2 %collective-permute-start.11 = (f32[2,1,32,2,128]{4,3,2,0,1:T(2,128)S(1)}, f32[2,1,32,2,128]{4,3,2,0,1:T(2,128)S(1)}, u32[]{:S(2)}, u32[]{:S(2)}) collective-permute-start(f32[2,1,32,2,128]{4,3,2,0,1:T(2,128)S(1)} %get-tuple-element.62), channel_id=1, source_target_pairs={{1,0},{2,1},{3,2},{4,3},{5,4},{6,5},{7,6},{8,7},{9,8},{10,9},{11,1... | collective-permute-start | bytes 196616 | tf_op jit(solution)/shard_map/ppermute | solution.py:15
  199.2 6.2 collective-permute-start.8
  202.8 5.2 collective-permute-start.9
  208.4 0.7 copy-start.10
  287.8 12.1 %collective-permute-start.14 = (f32[2,1,32,2,128]{4,3,2,0,1:T(2,128)S(1)}, f32[2,1,32,2,128]{4,3,2,0,1:T(2,128)S(1)}, u32[]{:S(2)}, u32[]{:S(2)}) collective-permute-start(f32[2,1,32,2,128]{4,3,2,0,1:T(2,128)S(1)} %get-tuple-element.55), channel_id=1, source_target_pairs={{0,1},{1,2},{2,3},{3,4},{4,5},{5,6},{6,7},{7,8},{8,9},{9,10},{10,1... | collective-permute-start | bytes 196616 | tf_op jit(solution)/shard_map/ppermute | solution.py:15
  289.7 10.2 %collective-permute-start.15 = (f32[2,1,32,2,128]{4,3,2,0,1:T(2,128)S(1)}, f32[2,1,32,2,128]{4,3,2,0,1:T(2,128)S(1)}, u32[]{:S(2)}, u32[]{:S(2)}) collective-permute-start(f32[2,1,32,2,128]{4,3,2,0,1:T(2,128)S(1)} %get-tuple-element.56), channel_id=1, source_target_pairs={{1,0},{2,1},{3,2},{4,3},{5,4},{6,5},{7,6},{8,7},{9,8},{10,9},{11,1... | collective-permute-start | bytes 196616 | tf_op jit(solution)/shard_map/ppermute | solution.py:15
  291.0 6.4 collective-permute-start.12
  294.7 5.2 collective-permute-start.13
  308.1 13.0 %collective-permute-start.18 = (f32[2,1,32,2,128]{4,3,2,0,1:T(2,128)S(1)}, f32[2,1,32,2,128]{4,3,2,0,1:T(2,128)S(1)}, u32[]{:S(2)}, u32[]{:S(2)}) collective-permute-start(f32[2,1,32,2,128]{4,3,2,0,1:T(2,128)S(1)} %get-tuple-element.49), channel_id=1, source_target_pairs={{0,1},{1,2},{2,3},{3,4},{4,5},{5,6},{6,7},{7,8},{8,9},{9,10},{10,1... | collective-permute-start | bytes 196616 | tf_op jit(solution)/shard_map/ppermute | solution.py:15
  312.4 8.7 %collective-permute-start.19 = (f32[2,1,32,2,128]{4,3,2,0,1:T(2,128)S(1)}, f32[2,1,32,2,128]{4,3,2,0,1:T(2,128)S(1)}, u32[]{:S(2)}, u32[]{:S(2)}) collective-permute-start(f32[2,1,32,2,128]{4,3,2,0,1:T(2,128)S(1)} %get-tuple-element.50), channel_id=1, source_target_pairs={{1,0},{2,1},{3,2},{4,3},{5,4},{6,5},{7,6},{8,7},{9,8},{10,9},{11,1... | collective-permute-start | bytes 196616 | tf_op jit(solution)/shard_map/ppermute | solution.py:15
  313.7 4.6 collective-permute-start.16
  315.9 5.2 collective-permute-start.17
  321.5 78.5 %copy-start.12 = (f32[2,1,32,8,128]{4,3,2,0,1:T(8,128)}, f32[2,1,32,8,128]{4,3,2,0,1:T(8,128)S(1)}, u32[]{:S(2)}) copy-start(f32[2,1,32,8,128]{4,3,2,0,1:T(8,128)S(1)} %convolution_bitcast_fusion.13) | copy-start | bytes 786436
  402.4 13.7 %copy-start.9 = (f32[2,1,32,8,128]{4,3,2,0,1:T(8,128)S(1)}, f32[2,1,32,8,128]{4,3,2,0,1:T(8,128)}, u32[]{:S(2)}) copy-start(f32[2,1,32,8,128]{4,3,2,0,1:T(8,128)} %copy-done.8) | copy-start | bytes 786436
  402.4 13.7 %copy-start.11 = (f32[2,1,32,8,128]{4,3,2,0,1:T(8,128)S(1)}, f32[2,1,32,8,128]{4,3,2,0,1:T(8,128)}, u32[]{:S(2)}) copy-start(f32[2,1,32,8,128]{4,3,2,0,1:T(8,128)} %copy-done.10) | copy-start | bytes 786436
  402.4 13.7 %copy-start.13 = (f32[2,1,32,8,128]{4,3,2,0,1:T(8,128)S(1)}, f32[2,1,32,8,128]{4,3,2,0,1:T(8,128)}, u32[]{:S(2)}) copy-start(f32[2,1,32,8,128]{4,3,2,0,1:T(8,128)} %copy-done.12) | copy-start | bytes 786436
  403.5 12.1 %collective-permute-start.22 = (f32[2,1,32,2,128]{4,3,2,0,1:T(2,128)S(1)}, f32[2,1,32,2,128]{4,3,2,0,1:T(2,128)S(1)}, u32[]{:S(2)}, u32[]{:S(2)}) collective-permute-start(f32[2,1,32,2,128]{4,3,2,0,1:T(2,128)S(1)} %get-tuple-element.43), channel_id=1, source_target_pairs={{0,1},{1,2},{2,3},{3,4},{4,5},{5,6},{6,7},{7,8},{8,9},{9,10},{10,1... | collective-permute-start | bytes 196616 | tf_op jit(solution)/shard_map/ppermute | solution.py:15
  405.4 10.2 %collective-permute-start.23 = (f32[2,1,32,2,128]{4,3,2,0,1:T(2,128)S(1)}, f32[2,1,32,2,128]{4,3,2,0,1:T(2,128)S(1)}, u32[]{:S(2)}, u32[]{:S(2)}) collective-permute-start(f32[2,1,32,2,128]{4,3,2,0,1:T(2,128)S(1)} %get-tuple-element.44), channel_id=1, source_target_pairs={{1,0},{2,1},{3,2},{4,3},{5,4},{6,5},{7,6},{8,7},{9,8},{10,9},{11,1... | collective-permute-start | bytes 196616 | tf_op jit(solution)/shard_map/ppermute | solution.py:15
  406.7 6.6 collective-permute-start.20
  410.3 5.2 collective-permute-start.21
  655.1 11.1 %collective-permute-start.26 = (f32[2,1,32,2,128]{4,3,2,0,1:T(2,128)S(1)}, f32[2,1,32,2,128]{4,3,2,0,1:T(2,128)S(1)}, u32[]{:S(2)}, u32[]{:S(2)}) collective-permute-start(f32[2,1,32,2,128]{4,3,2,0,1:T(2,128)S(1)} %get-tuple-element.37), channel_id=1, source_target_pairs={{0,1},{1,2},{2,3},{3,4},{4,5},{5,6},{6,7},{7,8},{8,9},{9,10},{10,1... | collective-permute-start | bytes 196616 | tf_op jit(solution)/shard_map/ppermute | solution.py:15
  656.9 9.3 %collective-permute-start.27 = (f32[2,1,32,2,128]{4,3,2,0,1:T(2,128)S(1)}, f32[2,1,32,2,128]{4,3,2,0,1:T(2,128)S(1)}, u32[]{:S(2)}, u32[]{:S(2)}) collective-permute-start(f32[2,1,32,2,128]{4,3,2,0,1:T(2,128)S(1)} %get-tuple-element.38), channel_id=1, source_target_pairs={{1,0},{2,1},{3,2},{4,3},{5,4},{6,5},{7,6},{8,7},{9,8},{10,9},{11,1... | collective-permute-start | bytes 196616 | tf_op jit(solution)/shard_map/ppermute | solution.py:15
  658.2 6.4 collective-permute-start.24
  661.0 5.2 collective-permute-start.25
  673.9 10.8 %copy-start.4 = (f32[2,1,32,8,128]{4,3,2,0,1:T(8,128)S(1)}, f32[2,1,32,8,128]{4,3,2,0,1:T(8,128)}, u32[]{:S(2)}) copy-start(f32[2,1,32,8,128]{4,3,2,0,1:T(8,128)} %copy-done.3) | copy-start | bytes 786436
  674.4 13.0 %collective-permute-start.30 = (f32[2,1,32,2,128]{4,3,2,0,1:T(2,128)S(1)}, f32[2,1,32,2,128]{4,3,2,0,1:T(2,128)S(1)}, u32[]{:S(2)}, u32[]{:S(2)}) collective-permute-start(f32[2,1,32,2,128]{4,3,2,0,1:T(2,128)S(1)} %get-tuple-element.31), channel_id=1, source_target_pairs={{0,1},{1,2},{2,3},{3,4},{4,5},{5,6},{6,7},{7,8},{8,9},{9,10},{10,1... | collective-permute-start | bytes 196616 | tf_op jit(solution)/shard_map/ppermute | solution.py:15
  678.7 8.7 %collective-permute-start.31 = (f32[2,1,32,2,128]{4,3,2,0,1:T(2,128)S(1)}, f32[2,1,32,2,128]{4,3,2,0,1:T(2,128)S(1)}, u32[]{:S(2)}, u32[]{:S(2)}) collective-permute-start(f32[2,1,32,2,128]{4,3,2,0,1:T(2,128)S(1)} %get-tuple-element.32), channel_id=1, source_target_pairs={{1,0},{2,1},{3,2},{4,3},{5,4},{6,5},{7,6},{8,7},{9,8},{10,9},{11,1... | collective-permute-start | bytes 196616 | tf_op jit(solution)/shard_map/ppermute | solution.py:15
  680.0 5.4 collective-permute-start.28
  682.2 5.2 collective-permute-start.29
  687.8 0.7 copy-start.6
  687.9 0.7 copy-start.1
  766.9 13.0 %copy-start.7 = (f32[2,1,32,8,128]{4,3,2,0,1:T(8,128)S(1)}, f32[2,1,32,8,128]{4,3,2,0,1:T(8,128)}, u32[]{:S(2)}) copy-start(f32[2,1,32,8,128]{4,3,2,0,1:T(8,128)} %copy-done.6) | copy-start | bytes 786436
  768.0 11.9 %collective-permute-start.34 = (f32[2,1,32,2,128]{4,3,2,0,1:T(2,128)S(1)}, f32[2,1,32,2,128]{4,3,2,0,1:T(2,128)S(1)}, u32[]{:S(2)}, u32[]{:S(2)}) collective-permute-start(f32[2,1,32,2,128]{4,3,2,0,1:T(2,128)S(1)} %get-tuple-element.25), channel_id=1, source_target_pairs={{0,1},{1,2},{2,3},{3,4},{4,5},{5,6},{6,7},{7,8},{8,9},{9,10},{10,1... | collective-permute-start | bytes 196616 | tf_op jit(solution)/shard_map/ppermute | solution.py:15
  769.7 10.2 %collective-permute-start.35 = (f32[2,1,32,2,128]{4,3,2,0,1:T(2,128)S(1)}, f32[2,1,32,2,128]{4,3,2,0,1:T(2,128)S(1)}, u32[]{:S(2)}, u32[]{:S(2)}) collective-permute-start(f32[2,1,32,2,128]{4,3,2,0,1:T(2,128)S(1)} %get-tuple-element.26), channel_id=1, source_target_pairs={{1,0},{2,1},{3,2},{4,3},{5,4},{6,5},{7,6},{8,7},{9,8},{10,9},{11,1... | collective-permute-start | bytes 196616 | tf_op jit(solution)/shard_map/ppermute | solution.py:15
  771.0 6.8 collective-permute-start.32
  774.7 5.2 collective-permute-start.33
  780.4 88.6 %copy-start.2 = (f32[2,32,1024]{2,1,0:T(8,128)S(1)}, f32[2,32,1024]{2,1,0:T(8,128)}, u32[]{:S(2)}) copy-start(f32[2,32,1024]{2,1,0:T(8,128)} %copy-done.1) | copy-start | bytes 786436
  780.4 89.6 %copy-start.5 = (f32[2,1,32,1024]{3,2,0,1:T(8,128)S(1)}, f32[2,1,32,1024]{3,2,0,1:T(8,128)}, u32[]{:S(2)}) copy-start(f32[2,1,32,1024]{3,2,0,1:T(8,128)} %reshape.472) | copy-start | bytes 786436
where the time goes:
time: 881 us; the launch traced here: 871 us
  blocking collectives  681 us (77%)
  starting transfers between devices  86.8 us (10%)
  matrix products  53.7 us (6%)
  waiting for transfers between devices  20.4 us (2%)
  other arithmetic  15.1 us (2%)
  local copies, waits for them, and re-layouts  12.1 us (1%)
    all_gather x6, blocking collectives, modes(): piece = lax.all_gather(mine, ('gx', 'gy'), axis=0, tiled=True)  446 us
    psum x2, blocking collectives, per_device(): lax.psum((inner(direction, image), inner(direction, resid)), ('gx', 'gy'))  161 us
    ppermute x36, starting transfers between devices, shifted(): lax.ppermute(value, axis, [(source, source + steps) for source in range(i...  86.8 us
    psum x1, blocking collectives, per_device(): cross_new = lax.psum(inner(image, resid), ('gx', 'gy'))  74.3 us
    dot_general x3, matrix products, applied(): return jnp.einsum('abrk,abkj->abrj', field, dual_operators, precision=HI)  21.6 us
    ppermute x36, waiting for transfers between devices, shifted(): lax.ppermute(value, axis, [(source, source + steps) for source in range(i...  20.4 us
  transfers between devices with their start and end apart: 36, of which 9 were waited for; matrix products, arithmetic and copies ran while one was open for 0% of the time, Pallas kernels for 0%

commit v1 on v0

--- a/solution.py
+++ b/solution.py
@@ -2,8 +2,6 @@
 import jax.numpy as jnp
 from jax import lax
 from jax.sharding import PartitionSpec as P
-
-ITERS = 2
 
 
 HI = lax.Precision.HIGHEST
@@ -35,6 +33,25 @@
     return lax.linalg.triangular_solve(lower, middle, left_side=True, lower=True, transpose_a=True)
 
 
+def spread_out(value, axis):
+    count = lax.axis_size(axis)
+    copies = jnp.broadcast_to(value, (count,) + value.shape)
+    return lax.all_to_all(copies, axis, 0, 0, tiled=False)
+
+
+def gather(rows):
+    across = spread_out(rows, "gy")
+    return spread_out(across.reshape(-1, 128), "gx").reshape(-1, 128)
+
+
+def gather_and_sum(rows, sums):
+    count = rows.shape[0]
+    both = spread_out(jnp.concatenate([rows, sums], 0), "gy")
+    part = both[:, :count].reshape(-1, 128)
+    both = spread_out(jnp.concatenate([part, both[:, count:].sum(0)], 0), "gx")
+    return both[:, : part.shape[0]].reshape(-1, 128), both[:, part.shape[0] :].sum(0)
+
+
 def per_device(
     dual_operators, rigid_trace, coarse_inverse, floating, block_map, interface_gap, rigid_load
 ):
@@ -49,7 +66,8 @@
     wblock = jnp.einsum("abqk,abq->abk", table, omega, precision=HI)
     wloc = jnp.repeat(wblock, rigid_trace.shape[3] // 8, axis=-1)
     live = floating.astype(jnp.float32)[:, :, None, None]
-    rows_local = coarse_inverse.reshape(coarse_inverse.shape[2], coarse_inverse.shape[3])
+    own, wide = coarse_inverse.shape[2], coarse_inverse.shape[3]
+    fold = coarse_inverse.reshape(own, wide // 4, 4).transpose(2, 0, 1).reshape(4 * own, wide // 4)
 
     def jump(field):
         subs, cols, width_cases, width = field.shape
@@ -68,19 +86,17 @@
     def inner(left, right):
         return jnp.einsum("abrk,absk->rs", left * wloc[:, :, None, :], right, precision=HI)
 
-    def modes(load):
-        mine = load.reshape(-1, load.shape[-1])
-        piece = lax.all_gather(mine, ("gx", "gy"), axis=0, tiled=True)
-        piece_rows = lax.slice_in_dim(rows_local, 0, piece.shape[0], axis=1)
-        alpha = jnp.zeros_like(mine) + jnp.dot(piece_rows, piece, precision=HI)
-        return alpha.reshape(load.shape) * live
+    def loads(field):
+        load = jnp.einsum("abmk,abrk->abmr", rigid_trace, field, precision=HI) * live
+        return load.reshape(-1, 128)
+
+    def modes(gathered):
+        product = jnp.dot(fold, gathered, precision=HI).reshape(4, own, 4, 32)
+        alpha = sum(product[q, :, q] for q in range(4))
+        return alpha.reshape(2, 1, -1, 32) * live
 
     def spread(alpha):
         return jump(jnp.einsum("abmr,abmk->abrk", alpha, rigid_trace, precision=HI))
-
-    def project(field):
-        load = jnp.einsum("abmk,abrk->abmr", rigid_trace, field, precision=HI) * live
-        return field - spread(modes(load))
 
     def applied(field):
         return jnp.einsum("abrk,abkj->abrj", field, dual_operators, precision=HI)
@@ -88,23 +104,45 @@
     def combine(field, mixing):
         return jnp.einsum("abrk,rs->absk", field, mixing, precision=HI)
 
-    solution = spread(modes(rigid_load * live))
-    resid = project(jump(interface_gap - applied(solution)))
-    direction = resid
-    for step in range(ITERS):
-        moved = project(direction)
-        image = project(jump(applied(moved)))
-        curvature, drive = lax.psum(
-            (inner(direction, image), inner(direction, resid)), ("gx", "gy")
-        )
-        step_len = chol_solve(curvature, drive)
-        solution = solution + combine(moved, step_len)
-        resid = resid - combine(image, step_len)
-        if step + 1 < ITERS:
-            cross_new = lax.psum(inner(image, resid), ("gx", "gy"))
-            coupling = chol_solve(curvature, cross_new)
-            direction = resid - combine(direction, coupling)
-    return (solution, resid)
+    def plain(left, right):
+        return jnp.einsum("abrk,absk->rs", left, right, precision=HI)
+
+    def packed(*grams):
+        return jnp.concatenate([gram.reshape(-1, 128) for gram in grams], 0)
+
+    start = modes(gather((rigid_load * live).reshape(-1, 128)))
+    first_solution = spread(start)
+    force = jump(interface_gap - applied(first_solution))
+    resid = force - spread(modes(gather(loads(force))))
+    alpha = modes(gather(loads(resid)))
+    moved = resid - spread(alpha)
+    pushed = applied(moved)
+    hit = jump(pushed)
+    gathered, grams = gather_and_sum(
+        loads(hit), packed(plain(moved, pushed), inner(resid, resid))
+    )
+    curvature, drive = grams.reshape(2, 32, 32)
+    image = hit - spread(modes(gathered))
+    step_len = chol_solve(curvature, drive)
+    next_resid = resid - combine(image, step_len)
+    gathered, grams = gather_and_sum(loads(image), packed(inner(image, next_resid)))
+    coupling = chol_solve(curvature, grams.reshape(32, 32))
+    direction = next_resid - combine(resid, coupling)
+    mix = jnp.eye(32, dtype=jnp.float32) - coupling
+    next_alpha = jnp.einsum("abmr,rs->abms", alpha, mix, precision=HI) - jnp.einsum(
+        "abmr,rs->abms", modes(gathered), step_len, precision=HI
+    )
+    next_moved = direction - spread(next_alpha)
+    pushed = applied(next_moved)
+    hit = jump(pushed)
+    gathered, grams = gather_and_sum(
+        loads(hit), packed(plain(next_moved, pushed), inner(direction, next_resid))
+    )
+    curvature, drive = grams.reshape(2, 32, 32)
+    image = hit - spread(modes(gathered))
+    next_step = chol_solve(curvature, drive)
+    solution = first_solution + combine(moved, step_len) + combine(next_moved, next_step)
+    return (solution, next_resid - combine(image, next_step))
 
 
 def solution(mesh):

time: 881 us -> 383 us (0.43)
  blocking collectives: 681 us -> 134 us
  starting transfers between devices: 86.8 us -> 129 us
  waiting for transfers between devices: 20.4 us -> 44.3 us
  matrix products: 53.7 us -> 43.2 us
    all_gather x6 -> x0, blocking collectives: 446 us -> none  [modes(): piece = lax.all_gather(mine, ('gx', 'gy'), axis=0, tiled=True)]
    psum x3 -> x0, blocking collectives: 235 us -> none  [the longest x2 161 us: per_device(): lax.psum((inner(direction, image), inner(direction, resid)), ('gx', 'gy'))]
    all_to_all x0 -> x7, blocking collectives: none -> 134 us  [spread_out(): return lax.all_to_all(copies, axis, 0, 0, tiled=False)]
    all_to_all x0 -> x5, waiting for transfers between devices: none -> 38.6 us  [spread_out(): return lax.all_to_all(copies, axis, 0, 0, tiled=False)]
    all_to_all x0 -> x5, starting transfers between devices: none -> 28 us  [spread_out(): return lax.all_to_all(copies, axis, 0, 0, tiled=False)]
    ppermute x36, waiting for transfers between devices: 20.4 us -> 5.62 us  [shifted(): lax.ppermute(value, axis, [(source, source + steps) for source in range(i...]
    ppermute x36, starting transfers between devices: 86.8 us -> 101 us  [shifted(): lax.ppermute(value, axis, [(source, source + steps) for source in range(i...]
    dot_general x11 -> x15, matrix products: 15.9 us -> 4.85 us  [the longest x6 2.08 us: modes(): product = jnp.dot(fold, gathered, precision=HI).reshape(4, own, 4, 32)]
  transfers between devices with their start and end apart: 36 -> 41, of which waited for: 9 -> 13; matrix products, arithmetic and copies ran while one was open for 0% -> 2% of each run, Pallas kernels for 0% -> 0%
where the time goes in v1:
time: 383 us; the launch traced here: 380 us
  blocking collectives  134 us (35%)
  starting transfers between devices  129 us (34%)
  waiting for transfers between devices  44.3 us (12%)
  matrix products  43.2 us (11%)
  other arithmetic  15.3 us (4%)
  local copies, waits for them, and re-layouts  11.9 us (3%)
    all_to_all x7, blocking collectives, spread_out(): return lax.all_to_all(copies, axis, 0, 0, tiled=False)  134 us
    ppermute x36, starting transfers between devices, shifted(): lax.ppermute(value, axis, [(source, source + steps) for source in range(i...  101 us
    all_to_all x5, waiting for transfers between devices, spread_out(): return lax.all_to_all(copies, axis, 0, 0, tiled=False)  38.6 us
    all_to_all x5, starting transfers between devices, spread_out(): return lax.all_to_all(copies, axis, 0, 0, tiled=False)  28 us
    dot_general x3, matrix products, applied(): return jnp.einsum('abrk,abkj->abrj', field, dual_operators, precision=HI)  21.5 us
  transfers between devices with their start and end apart: 41, of which 13 were waited for; matrix products, arithmetic and copies ran while one was open for 2% of the time, Pallas kernels for 0%

profile of v1, /device:TPU:1, one launch (start us, length us, event | category | flops | bytes accessed | tf_op | source)
XLA Modules:
  0.0 380.4 jit_solution(4430967460798873484)
XLA Ops:
  2.2 20.5 %all_to_all.60 = f32[32,3,128]{2,1,0:T(4,128)S(1)} all-to-all(f32[32,3,128]{2,1,0:T(4,128)S(1)} %broadcast_in_dim.60), channel_id=1, replica_groups=mesh['gx'=8,'gy'=32] {'gy'}, dimensions={0} | all-to-all | bytes 98304 | tf_op jit(solution)/shard_map/all_to_all | solution.py:39
  23.5 6.6 %all-to-all-start.1 = ((f32[8,96,128]{2,1,0:T(8,128)}), f32[8,96,128]{2,1,0:T(8,128)S(1)}, u32[]{:S(2)}, u32[]{:S(2)}) async-start(f32[8,96,128]{2,1,0:T(8,128)} %broadcast_in_dim.61), calls=%async_computation.1 | async-start | bytes 786432 | tf_op jit(solution)/shard_map/all_to_all | solution.py:39
  30.9 1.4 copy.89
  33.0 5.1 %all-to-all-done.1 = f32[8,96,128]{2,1,0:T(8,128)S(1)} async-done(((f32[8,96,128]{2,1,0:T(8,128)}), f32[8,96,128]{2,1,0:T(8,128)S(1)}, u32[]{:S(2)}, u32[]{:S(2)}) %all-to-all-start.1) | async-done | bytes 393248 | tf_op jit(solution)/shard_map/all_to_all | solution.py:39
  39.2 1.1 convolution_bitcast_fusion.22
  40.4 1.3 collective-permute-start.3
  41.7 4.0 %collective-permute-start.2 = (f32[2,1,32,2,128]{4,3,2,0,1:T(2,128)S(1)}, f32[2,1,32,2,128]{4,3,2,0,1:T(2,128)S(1)}, u32[]{:S(2)}, u32[]{:S(2)}) collective-permute-start(f32[2,1,32,2,128]{4,3,2,0,1:T(2,128)S(1)} %get-tuple-element.65), channel_id=1, source_target_pairs={{0,1},{1,2},{2,3},{3,4},{4,5},{5,6},{6,7},{7,8},{8,9},{9,10},{10,1... | collective-permute-start | bytes 196616 | tf_op jit(solution)/shard_map/ppermute | solution.py:13
  45.7 3.3 collective-permute-start.1
  49.0 2.2 collective-permute-start
  53.4 7.2 %fusion.16 = f32[2,1,32,1024]{3,2,0,1:T(8,128)S(1)} fusion(f32[2,32,1024]{2,1,0:T(8,128)S(1)} %reshape.628, f32[2,1,1024,1024]{3,2,1,0:T(8,128)} %param.12, f32[2,1,32,1024]{3,2,1,0:T(8,128)S(1)} %copy-done), kind=kOutput, calls=%fused_computation.37 | convolution fusion | flops 805371904 | bytes 9175040 | tf_op jit(solution)/shard_map/abrk,abkj->abrj/dot_general | solution.py:102
  61.1 1.3 collective-permute-start.7
  62.4 4.0 %collective-permute-start.6 = (f32[2,1,32,2,128]{4,3,2,0,1:T(2,128)S(1)}, f32[2,1,32,2,128]{4,3,2,0,1:T(2,128)S(1)}, u32[]{:S(2)}, u32[]{:S(2)}) collective-permute-start(f32[2,1,32,2,128]{4,3,2,0,1:T(2,128)S(1)} %get-tuple-element.59), channel_id=1, source_target_pairs={{0,1},{1,2},{2,3},{3,4},{4,5},{5,6},{6,7},{7,8},{8,9},{9,10},{10,1... | collective-permute-start | bytes 196616 | tf_op jit(solution)/shard_map/ppermute | solution.py:13
  66.5 2.5 collective-permute-start.5
  69.0 4.2 %collective-permute-start.4 = (f32[1,1,32,2,128]{4,3,2,0,1:T(2,128)S(1)}, f32[1,1,32,2,128]{4,3,2,0,1:T(2,128)S(1)}, u32[]{:S(2)}, u32[]{:S(2)}) collective-permute-start(f32[1,1,32,2,128]{4,3,2,0,1:T(2,128)S(1)} %get-tuple-element.55), channel_id=1, source_target_pairs={{0,32},{32,64},{64,96},{96,128},{128,160},{160,192},{192,224},{1,3... | collective-permute-start | bytes 98312 | tf_op jit(solution)/shard_map/ppermute | solution.py:13
  75.1 18.3 %all_to_all.61 = f32[32,3,128]{2,1,0:T(4,128)S(1)} all-to-all(f32[32,3,128]{2,1,0:T(4,128)S(1)} %broadcast_in_dim.62), channel_id=1, replica_groups=mesh['gx'=8,'gy'=32] {'gy'}, dimensions={0} | all-to-all | bytes 98304 | tf_op jit(solution)/shard_map/all_to_all | solution.py:39
  93.4 13.9 %all_to_all.62 = f32[8,96,128]{2,1,0:T(8,128)S(1)} all-to-all(f32[8,96,128]{2,1,0:T(8,128)S(1)} %broadcast_in_dim.63), channel_id=1, replica_groups=mesh['gx'=8,'gy'=32] {'gx'}, dimensions={0} | all-to-all | bytes 786432 | tf_op jit(solution)/shard_map/all_to_all | solution.py:39
  108.9 1.3 collective-permute-start.11
  110.2 4.0 %collective-permute-start.10 = (f32[2,1,32,2,128]{4,3,2,0,1:T(2,128)S(1)}, f32[2,1,32,2,128]{4,3,2,0,1:T(2,128)S(1)}, u32[]{:S(2)}, u32[]{:S(2)}) collective-permute-start(f32[2,1,32,2,128]{4,3,2,0,1:T(2,128)S(1)} %get-tuple-element.53), channel_id=1, source_target_pairs={{0,1},{1,2},{2,3},{3,4},{4,5},{5,6},{6,7},{7,8},{8,9},{9,10},{10,1... | collective-permute-start | bytes 196616 | tf_op jit(solution)/shard_map/ppermute | solution.py:13
  114.2 3.3 collective-permute-start.9
  117.6 2.2 collective-permute-start.8
  121.7 15.1 %all_to_all.63 = f32[32,3,128]{2,1,0:T(4,128)S(1)} all-to-all(f32[32,3,128]{2,1,0:T(4,128)S(1)} %broadcast_in_dim.64), channel_id=1, replica_groups=mesh['gx'=8,'gy'=32] {'gy'}, dimensions={0} | all-to-all | bytes 98304 | tf_op jit(solution)/shard_map/all_to_all | solution.py:39
  137.6 5.9 %all-to-all-start.5 = ((f32[8,96,128]{2,1,0:T(8,128)}), f32[8,96,128]{2,1,0:T(8,128)S(1)}, u32[]{:S(2)}, u32[]{:S(2)}) async-start(f32[8,96,128]{2,1,0:T(8,128)} %broadcast_in_dim.65), calls=%async_computation.5 | async-start | bytes 786432 | tf_op jit(solution)/shard_map/all_to_all | solution.py:39
  143.9 7.7 %all-to-all-done.5 = f32[8,96,128]{2,1,0:T(8,128)S(1)} async-done(((f32[8,96,128]{2,1,0:T(8,128)}), f32[8,96,128]{2,1,0:T(8,128)S(1)}, u32[]{:S(2)}, u32[]{:S(2)}) %all-to-all-start.5) | async-done | bytes 393248 | tf_op jit(solution)/shard_map/all_to_all | solution.py:39
  153.2 1.3 collective-permute-start.15
  154.5 4.0 %collective-permute-start.14 = (f32[2,1,32,2,128]{4,3,2,0,1:T(2,128)S(1)}, f32[2,1,32,2,128]{4,3,2,0,1:T(2,128)S(1)}, u32[]{:S(2)}, u32[]{:S(2)}) collective-permute-start(f32[2,1,32,2,128]{4,3,2,0,1:T(2,128)S(1)} %get-tuple-element.47), channel_id=1, source_target_pairs={{0,1},{1,2},{2,3},{3,4},{4,5},{5,6},{6,7},{7,8},{8,9},{9,10},{10,1... | collective-permute-start | bytes 196616 | tf_op jit(solution)/shard_map/ppermute | solution.py:13
  158.5 3.4 collective-permute-start.13
  161.8 2.4 collective-permute-start.12
  165.5 7.2 %fusion.2 = f32[2,32,1024]{2,1,0:T(8,128)S(1)} fusion(f32[2,32,1024]{2,1,0:T(8,128)S(1)} %sub.114, f32[2,1,1024,1024]{3,2,1,0:T(8,128)} %param.12), kind=kOutput, calls=%fused_computation.2 | convolution fusion | flops 805306368 | bytes 8912896 | tf_op jit(solution)/shard_map/abrk,abkj->abrj/dot_general | solution.py:102
  173.7 1.3 collective-permute-start.19
  175.0 4.0 %collective-permute-start.18 = (f32[2,1,32,2,128]{4,3,2,0,1:T(2,128)S(1)}, f32[2,1,32,2,128]{4,3,2,0,1:T(2,128)S(1)}, u32[]{:S(2)}, u32[]{:S(2)}) collective-permute-start(f32[2,1,32,2,128]{4,3,2,0,1:T(2,128)S(1)} %get-tuple-element.41), channel_id=1, source_target_pairs={{0,1},{1,2},{2,3},{3,4},{4,5},{5,6},{6,7},{7,8},{8,9},{9,10},{10,1... | collective-permute-start | bytes 196616 | tf_op jit(solution)/shard_map/ppermute | solution.py:13
  179.0 2.5 collective-permute-start.17
  181.5 4.2 %collective-permute-start.16 = (f32[1,1,32,2,128]{4,3,2,0,1:T(2,128)S(1)}, f32[1,1,32,2,128]{4,3,2,0,1:T(2,128)S(1)}, u32[]{:S(2)}, u32[]{:S(2)}) collective-permute-start(f32[1,1,32,2,128]{4,3,2,0,1:T(2,128)S(1)} %get-tuple-element.37), channel_id=1, source_target_pairs={{0,32},{32,64},{64,96},{96,128},{128,160},{160,192},{192,224},{1,3... | collective-permute-start | bytes 98312 | tf_op jit(solution)/shard_map/ppermute | solution.py:13
  187.6 23.8 %all_to_all.64 = f32[32,19,128]{2,1,0:T(8,128)S(1)} all-to-all(f32[32,19,128]{2,1,0:T(8,128)S(1)} %broadcast_in_dim.69), channel_id=1, replica_groups=mesh['gx'=8,'gy'=32] {'gy'}, dimensions={0} | all-to-all | bytes 622592 | tf_op jit(solution)/shard_map/all_to_all | solution.py:39
  212.3 5.1 %all-to-all-start.7 = ((f32[8,112,128]{2,1,0:T(8,128)}), f32[8,112,128]{2,1,0:T(8,128)S(1)}, u32[]{:S(2)}, u32[]{:S(2)}) async-start(f32[8,112,128]{2,1,0:T(8,128)} %broadcast_in_dim.70), calls=%async_computation.7 | async-start | bytes 917504 | tf_op jit(solution)/shard_map/all_to_all | solution.py:39
  217.5 8.7 %all-to-all-done.7 = f32[8,112,128]{2,1,0:T(8,128)S(1)} async-done(((f32[8,112,128]{2,1,0:T(8,128)}), f32[8,112,128]{2,1,0:T(8,128)S(1)}, u32[]{:S(2)}, u32[]{:S(2)}) %all-to-all-start.7) | async-done | bytes 458784 | tf_op jit(solution)/shard_map/all_to_all | solution.py:39
  228.1 2.9 cholesky.44
  232.3 2.4 custom-call.13
  234.8 1.3 collective-permute-start.23
  236.1 4.0 %collective-permute-start.22 = (f32[2,1,32,2,128]{4,3,2,0,1:T(2,128)S(1)}, f32[2,1,32,2,128]{4,3,2,0,1:T(2,128)S(1)}, u32[]{:S(2)}, u32[]{:S(2)}) collective-permute-start(f32[2,1,32,2,128]{4,3,2,0,1:T(2,128)S(1)} %get-tuple-element.35), channel_id=1, source_target_pairs={{0,1},{1,2},{2,3},{3,4},{4,5},{5,6},{6,7},{7,8},{8,9},{9,10},{10,1... | collective-permute-start | bytes 196616 | tf_op jit(solution)/shard_map/ppermute | solution.py:13
  240.1 3.4 collective-permute-start.21
  243.4 2.2 collective-permute-start.20
  248.5 18.5 %all_to_all.65 = f32[32,11,128]{2,1,0:T(8,128)S(1)} all-to-all(f32[32,11,128]{2,1,0:T(8,128)S(1)} %broadcast_in_dim.71), channel_id=1, replica_groups=mesh['gx'=8,'gy'=32] {'gy'}, dimensions={0} | all-to-all | bytes 360448 | tf_op jit(solution)/shard_map/all_to_all | solution.py:39
  267.9 5.4 %all-to-all-start.9 = ((f32[8,104,128]{2,1,0:T(8,128)}), f32[8,104,128]{2,1,0:T(8,128)S(1)}, u32[]{:S(2)}, u32[]{:S(2)}) async-start(f32[8,104,128]{2,1,0:T(8,128)} %broadcast_in_dim.72), calls=%async_computation.9 | async-start | bytes 851968 | tf_op jit(solution)/shard_map/all_to_all | solution.py:39
  273.3 8.4 %all-to-all-done.9 = f32[8,104,128]{2,1,0:T(8,128)S(1)} async-done(((f32[8,104,128]{2,1,0:T(8,128)}), f32[8,104,128]{2,1,0:T(8,128)S(1)}, u32[]{:S(2)}, u32[]{:S(2)}) %all-to-all-start.9) | async-done | bytes 426016 | tf_op jit(solution)/shard_map/all_to_all | solution.py:39
  284.6 1.3 collective-permute-start.27
  285.9 4.0 %collective-permute-start.26 = (f32[2,1,32,2,128]{4,3,2,0,1:T(2,128)S(1)}, f32[2,1,32,2,128]{4,3,2,0,1:T(2,128)S(1)}, u32[]{:S(2)}, u32[]{:S(2)}) collective-permute-start(f32[2,1,32,2,128]{4,3,2,0,1:T(2,128)S(1)} %get-tuple-element.29), channel_id=1, source_target_pairs={{0,1},{1,2},{2,3},{3,4},{4,5},{5,6},{6,7},{7,8},{8,9},{9,10},{10,1... | collective-permute-start | bytes 196616 | tf_op jit(solution)/shard_map/ppermute | solution.py:13
  289.9 3.3 collective-permute-start.25
  293.2 2.4 collective-permute-start.24
  296.9 7.2 %fusion = f32[2,32,1024]{2,1,0:T(8,128)S(1)} fusion(f32[2,1,1024,1024]{3,2,1,0:T(8,128)} %param.12, f32[2,1,32,1024]{3,2,0,1:T(8,128)S(1)} %fusion.13, f32[2,1,32,1024]{3,2,0,1:T(8,128)S(1)} %reshape.670), kind=kOutput, calls=%fused_computation | convolution fusion | flops 805371904 | bytes 9175040 | tf_op jit(solution)/shard_map/abrk,abkj->abrj/dot_general | solution.py:102
  304.6 1.3 collective-permute-start.31
  305.9 4.0 %collective-permute-start.30 = (f32[2,1,32,2,128]{4,3,2,0,1:T(2,128)S(1)}, f32[2,1,32,2,128]{4,3,2,0,1:T(2,128)S(1)}, u32[]{:S(2)}, u32[]{:S(2)}) collective-permute-start(f32[2,1,32,2,128]{4,3,2,0,1:T(2,128)S(1)} %get-tuple-element.23), channel_id=1, source_target_pairs={{0,1},{1,2},{2,3},{3,4},{4,5},{5,6},{6,7},{7,8},{8,9},{9,10},{10,1... | collective-permute-start | bytes 196616 | tf_op jit(solution)/shard_map/ppermute | solution.py:13
  309.9 2.5 collective-permute-start.29
  312.4 4.2 %collective-permute-start.28 = (f32[1,1,32,2,128]{4,3,2,0,1:T(2,128)S(1)}, f32[1,1,32,2,128]{4,3,2,0,1:T(2,128)S(1)}, u32[]{:S(2)}, u32[]{:S(2)}) collective-permute-start(f32[1,1,32,2,128]{4,3,2,0,1:T(2,128)S(1)} %get-tuple-element.19), channel_id=1, source_target_pairs={{0,32},{32,64},{64,96},{96,128},{128,160},{160,192},{192,224},{1,3... | collective-permute-start | bytes 98312 | tf_op jit(solution)/shard_map/ppermute | solution.py:13
  318.6 24.1 %all_to_all.66 = f32[32,19,128]{2,1,0:T(8,128)S(1)} all-to-all(f32[32,19,128]{2,1,0:T(8,128)S(1)} %broadcast_in_dim.75), channel_id=1, replica_groups=mesh['gx'=8,'gy'=32] {'gy'}, dimensions={0} | all-to-all | bytes 622592 | tf_op jit(solution)/shard_map/all_to_all | solution.py:39
  343.6 5.1 %all-to-all-start.11 = ((f32[8,112,128]{2,1,0:T(8,128)}), f32[8,112,128]{2,1,0:T(8,128)S(1)}, u32[]{:S(2)}, u32[]{:S(2)}) async-start(f32[8,112,128]{2,1,0:T(8,128)} %broadcast_in_dim.76), calls=%async_computation.11 | async-start | bytes 917504 | tf_op jit(solution)/shard_map/all_to_all | solution.py:39
  348.7 8.7 %all-to-all-done.11 = f32[8,112,128]{2,1,0:T(8,128)S(1)} async-done(((f32[8,112,128]{2,1,0:T(8,128)}), f32[8,112,128]{2,1,0:T(8,128)S(1)}, u32[]{:S(2)}, u32[]{:S(2)}) %all-to-all-start.11) | async-done | bytes 458784 | tf_op jit(solution)/shard_map/all_to_all | solution.py:39
  359.3 2.9 cholesky.55
  363.6 2.4 custom-call.17
  366.8 1.3 collective-permute-start.35
  368.1 4.0 %collective-permute-start.34 = (f32[2,1,32,2,128]{4,3,2,0,1:T(2,128)S(1)}, f32[2,1,32,2,128]{4,3,2,0,1:T(2,128)S(1)}, u32[]{:S(2)}, u32[]{:S(2)}) collective-permute-start(f32[2,1,32,2,128]{4,3,2,0,1:T(2,128)S(1)} %get-tuple-element.17), channel_id=1, source_target_pairs={{0,1},{1,2},{2,3},{3,4},{4,5},{5,6},{6,7},{7,8},{8,9},{9,10},{10,1... | collective-permute-start | bytes 196616 | tf_op jit(solution)/shard_map/ppermute | solution.py:13
  372.1 3.3 collective-permute-start.33
  375.5 2.2 collective-permute-start.32
  377.7 1.1 fusion.11
  379.3 1.1 fusion.15
  (235 shorter events, 39.1 us)
Async XLA Ops:
  0.6 52.8 %copy-start = (f32[2,1,32,1024]{3,2,1,0:T(8,128)S(1)}, f32[2,1,32,1024]{3,2,1,0:T(8,128)}, u32[]{:S(2)}) copy-start(f32[2,1,32,1024]{3,2,1,0:T(8,128)} %param.17) | copy-start | bytes 786436
  23.5 14.6 %all-to-all-start.1 = ((f32[8,96,128]{2,1,0:T(8,128)}), f32[8,96,128]{2,1,0:T(8,128)S(1)}, u32[]{:S(2)}, u32[]{:S(2)}) async-start(f32[8,96,128]{2,1,0:T(8,128)} %broadcast_in_dim.61), calls=%async_computation.1 | async-start | bytes 786432 | tf_op jit(solution)/shard_map/all_to_all | solution.py:39
  30.9 29.8 %copy-start.1 = (s32[2,1,8]{2,1,0:T(1,128)S(1)}, s32[2,1,8]{2,1,0:T(1,128)}, u32[]{:S(2)}) copy-start(s32[2,1,8]{2,1,0:T(1,128)} %param.16) | copy-start | bytes 196
  40.4 11.9 %collective-permute-start.3 = (f32[2,1,32,2,128]{4,3,2,0,1:T(2,128)S(1)}, f32[2,1,32,2,128]{4,3,2,0,1:T(2,128)S(1)}, u32[]{:S(2)}, u32[]{:S(2)}) collective-permute-start(f32[2,1,32,2,128]{4,3,2,0,1:T(2,128)S(1)} %get-tuple-element.66), channel_id=1, source_target_pairs={{1,0},{2,1},{3,2},{4,3},{5,4},{6,5},{7,6},{8,7},{9,8},{10,9},{11,1... | collective-permute-start | bytes 196616 | tf_op jit(solution)/shard_map/ppermute | solution.py:13
  41.7 10.6 %collective-permute-start.2 = (f32[2,1,32,2,128]{4,3,2,0,1:T(2,128)S(1)}, f32[2,1,32,2,128]{4,3,2,0,1:T(2,128)S(1)}, u32[]{:S(2)}, u32[]{:S(2)}) collective-permute-start(f32[2,1,32,2,128]{4,3,2,0,1:T(2,128)S(1)} %get-tuple-element.65), channel_id=1, source_target_pairs={{0,1},{1,2},{2,3},{3,4},{4,5},{5,6},{6,7},{7,8},{8,9},{9,10},{10,1... | collective-permute-start | bytes 196616 | tf_op jit(solution)/shard_map/ppermute | solution.py:13
  45.7 5.6 %collective-permute-start.1 = (f32[1,1,32,2,128]{4,3,2,0,1:T(2,128)S(1)}, f32[1,1,32,2,128]{4,3,2,0,1:T(2,128)S(1)}, u32[]{:S(2)}, u32[]{:S(2)}) collective-permute-start(f32[1,1,32,2,128]{4,3,2,0,1:T(2,128)S(1)} %get-tuple-element.62), channel_id=1, source_target_pairs={{32,0},{64,32},{96,64},{128,96},{160,128},{192,160},{224,192},{33,... | collective-permute-start | bytes 98312 | tf_op jit(solution)/shard_map/ppermute | solution.py:13
  49.0 3.2 collective-permute-start
  61.1 13.1 %collective-permute-start.7 = (f32[2,1,32,2,128]{4,3,2,0,1:T(2,128)S(1)}, f32[2,1,32,2,128]{4,3,2,0,1:T(2,128)S(1)}, u32[]{:S(2)}, u32[]{:S(2)}) collective-permute-start(f32[2,1,32,2,128]{4,3,2,0,1:T(2,128)S(1)} %get-tuple-element.60), channel_id=1, source_target_pairs={{1,0},{2,1},{3,2},{4,3},{5,4},{6,5},{7,6},{8,7},{9,8},{10,9},{11,1... | collective-permute-start | bytes 196616 | tf_op jit(solution)/shard_map/ppermute | solution.py:13
  62.4 11.8 %collective-permute-start.6 = (f32[2,1,32,2,128]{4,3,2,0,1:T(2,128)S(1)}, f32[2,1,32,2,128]{4,3,2,0,1:T(2,128)S(1)}, u32[]{:S(2)}, u32[]{:S(2)}) collective-permute-start(f32[2,1,32,2,128]{4,3,2,0,1:T(2,128)S(1)} %get-tuple-element.59), channel_id=1, source_target_pairs={{0,1},{1,2},{2,3},{3,4},{4,5},{5,6},{6,7},{7,8},{8,9},{9,10},{10,1... | collective-permute-start | bytes 196616 | tf_op jit(solution)/shard_map/ppermute | solution.py:13
  66.5 6.7 %collective-permute-start.5 = (f32[1,1,32,2,128]{4,3,2,0,1:T(2,128)S(1)}, f32[1,1,32,2,128]{4,3,2,0,1:T(2,128)S(1)}, u32[]{:S(2)}, u32[]{:S(2)}) collective-permute-start(f32[1,1,32,2,128]{4,3,2,0,1:T(2,128)S(1)} %get-tuple-element.56), channel_id=1, source_target_pairs={{32,0},{64,32},{96,64},{128,96},{160,128},{192,160},{224,192},{33,... | collective-permute-start | bytes 98312 | tf_op jit(solution)/shard_map/ppermute | solution.py:13
  69.0 5.2 %collective-permute-start.4 = (f32[1,1,32,2,128]{4,3,2,0,1:T(2,128)S(1)}, f32[1,1,32,2,128]{4,3,2,0,1:T(2,128)S(1)}, u32[]{:S(2)}, u32[]{:S(2)}) collective-permute-start(f32[1,1,32,2,128]{4,3,2,0,1:T(2,128)S(1)} %get-tuple-element.55), channel_id=1, source_target_pairs={{0,32},{32,64},{64,96},{96,128},{128,160},{160,192},{192,224},{1,3... | collective-permute-start | bytes 98312 | tf_op jit(solution)/shard_map/ppermute | solution.py:13
  108.9 11.9 %collective-permute-start.11 = (f32[2,1,32,2,128]{4,3,2,0,1:T(2,128)S(1)}, f32[2,1,32,2,128]{4,3,2,0,1:T(2,128)S(1)}, u32[]{:S(2)}, u32[]{:S(2)}) collective-permute-start(f32[2,1,32,2,128]{4,3,2,0,1:T(2,128)S(1)} %get-tuple-element.54), channel_id=1, source_target_pairs={{1,0},{2,1},{3,2},{4,3},{5,4},{6,5},{7,6},{8,7},{9,8},{10,9},{11,1... | collective-permute-start | bytes 196616 | tf_op jit(solution)/shard_map/ppermute | solution.py:13
  110.2 10.6 %collective-permute-start.10 = (f32[2,1,32,2,128]{4,3,2,0,1:T(2,128)S(1)}, f32[2,1,32,2,128]{4,3,2,0,1:T(2,128)S(1)}, u32[]{:S(2)}, u32[]{:S(2)}) collective-permute-start(f32[2,1,32,2,128]{4,3,2,0,1:T(2,128)S(1)} %get-tuple-element.53), channel_id=1, source_target_pairs={{0,1},{1,2},{2,3},{3,4},{4,5},{5,6},{6,7},{7,8},{8,9},{9,10},{10,1... | collective-permute-start | bytes 196616 | tf_op jit(solution)/shard_map/ppermute | solution.py:13
  114.2 5.6 %collective-permute-start.9 = (f32[1,1,32,2,128]{4,3,2,0,1:T(2,128)S(1)}, f32[1,1,32,2,128]{4,3,2,0,1:T(2,128)S(1)}, u32[]{:S(2)}, u32[]{:S(2)}) collective-permute-start(f32[1,1,32,2,128]{4,3,2,0,1:T(2,128)S(1)} %get-tuple-element.50), channel_id=1, source_target_pairs={{32,0},{64,32},{96,64},{128,96},{160,128},{192,160},{224,192},{33,... | collective-permute-start | bytes 98312 | tf_op jit(solution)/shard_map/ppermute | solution.py:13
  117.6 3.2 collective-permute-start.8
  137.6 14.0 %all-to-all-start.5 = ((f32[8,96,128]{2,1,0:T(8,128)}), f32[8,96,128]{2,1,0:T(8,128)S(1)}, u32[]{:S(2)}, u32[]{:S(2)}) async-start(f32[8,96,128]{2,1,0:T(8,128)} %broadcast_in_dim.65), calls=%async_computation.5 | async-start | bytes 786432 | tf_op jit(solution)/shard_map/all_to_all | solution.py:39
  153.2 11.9 %collective-permute-start.15 = (f32[2,1,32,2,128]{4,3,2,0,1:T(2,128)S(1)}, f32[2,1,32,2,128]{4,3,2,0,1:T(2,128)S(1)}, u32[]{:S(2)}, u32[]{:S(2)}) collective-permute-start(f32[2,1,32,2,128]{4,3,2,0,1:T(2,128)S(1)} %get-tuple-element.48), channel_id=1, source_target_pairs={{1,0},{2,1},{3,2},{4,3},{5,4},{6,5},{7,6},{8,7},{9,8},{10,9},{11,1... | collective-permute-start | bytes 196616 | tf_op jit(solution)/shard_map/ppermute | solution.py:13
  154.5 10.6 %collective-permute-start.14 = (f32[2,1,32,2,128]{4,3,2,0,1:T(2,128)S(1)}, f32[2,1,32,2,128]{4,3,2,0,1:T(2,128)S(1)}, u32[]{:S(2)}, u32[]{:S(2)}) collective-permute-start(f32[2,1,32,2,128]{4,3,2,0,1:T(2,128)S(1)} %get-tuple-element.47), channel_id=1, source_target_pairs={{0,1},{1,2},{2,3},{3,4},{4,5},{5,6},{6,7},{7,8},{8,9},{9,10},{10,1... | collective-permute-start | bytes 196616 | tf_op jit(solution)/shard_map/ppermute | solution.py:13
  158.5 6.0 %collective-permute-start.13 = (f32[1,1,32,2,128]{4,3,2,0,1:T(2,128)S(1)}, f32[1,1,32,2,128]{4,3,2,0,1:T(2,128)S(1)}, u32[]{:S(2)}, u32[]{:S(2)}) collective-permute-start(f32[1,1,32,2,128]{4,3,2,0,1:T(2,128)S(1)} %get-tuple-element.44), channel_id=1, source_target_pairs={{32,0},{64,32},{96,64},{128,96},{160,128},{192,160},{224,192},{33,... | collective-permute-start | bytes 98312 | tf_op jit(solution)/shard_map/ppermute | solution.py:13
  161.8 3.2 collective-permute-start.12
  173.7 13.0 %collective-permute-start.19 = (f32[2,1,32,2,128]{4,3,2,0,1:T(2,128)S(1)}, f32[2,1,32,2,128]{4,3,2,0,1:T(2,128)S(1)}, u32[]{:S(2)}, u32[]{:S(2)}) collective-permute-start(f32[2,1,32,2,128]{4,3,2,0,1:T(2,128)S(1)} %get-tuple-element.42), channel_id=1, source_target_pairs={{1,0},{2,1},{3,2},{4,3},{5,4},{6,5},{7,6},{8,7},{9,8},{10,9},{11,1... | collective-permute-start | bytes 196616 | tf_op jit(solution)/shard_map/ppermute | solution.py:13
  175.0 11.7 %collective-permute-start.18 = (f32[2,1,32,2,128]{4,3,2,0,1:T(2,128)S(1)}, f32[2,1,32,2,128]{4,3,2,0,1:T(2,128)S(1)}, u32[]{:S(2)}, u32[]{:S(2)}) collective-permute-start(f32[2,1,32,2,128]{4,3,2,0,1:T(2,128)S(1)} %get-tuple-element.41), channel_id=1, source_target_pairs={{0,1},{1,2},{2,3},{3,4},{4,5},{5,6},{6,7},{7,8},{8,9},{9,10},{10,1... | collective-permute-start | bytes 196616 | tf_op jit(solution)/shard_map/ppermute | solution.py:13
  179.0 7.3 %collective-permute-start.17 = (f32[1,1,32,2,128]{4,3,2,0,1:T(2,128)S(1)}, f32[1,1,32,2,128]{4,3,2,0,1:T(2,128)S(1)}, u32[]{:S(2)}, u32[]{:S(2)}) collective-permute-start(f32[1,1,32,2,128]{4,3,2,0,1:T(2,128)S(1)} %get-tuple-element.38), channel_id=1, source_target_pairs={{32,0},{64,32},{96,64},{128,96},{160,128},{192,160},{224,192},{33,... | collective-permute-start | bytes 98312 | tf_op jit(solution)/shard_map/ppermute | solution.py:13
  181.5 5.2 %collective-permute-start.16 = (f32[1,1,32,2,128]{4,3,2,0,1:T(2,128)S(1)}, f32[1,1,32,2,128]{4,3,2,0,1:T(2,128)S(1)}, u32[]{:S(2)}, u32[]{:S(2)}) collective-permute-start(f32[1,1,32,2,128]{4,3,2,0,1:T(2,128)S(1)} %get-tuple-element.37), channel_id=1, source_target_pairs={{0,32},{32,64},{64,96},{96,128},{128,160},{160,192},{192,224},{1,3... | collective-permute-start | bytes 98312 | tf_op jit(solution)/shard_map/ppermute | solution.py:13
  212.3 13.9 %all-to-all-start.7 = ((f32[8,112,128]{2,1,0:T(8,128)}), f32[8,112,128]{2,1,0:T(8,128)S(1)}, u32[]{:S(2)}, u32[]{:S(2)}) async-start(f32[8,112,128]{2,1,0:T(8,128)} %broadcast_in_dim.70), calls=%async_computation.7 | async-start | bytes 917504 | tf_op jit(solution)/shard_map/all_to_all | solution.py:39
  234.8 11.9 %collective-permute-start.23 = (f32[2,1,32,2,128]{4,3,2,0,1:T(2,128)S(1)}, f32[2,1,32,2,128]{4,3,2,0,1:T(2,128)S(1)}, u32[]{:S(2)}, u32[]{:S(2)}) collective-permute-start(f32[2,1,32,2,128]{4,3,2,0,1:T(2,128)S(1)} %get-tuple-element.36), channel_id=1, source_target_pairs={{1,0},{2,1},{3,2},{4,3},{5,4},{6,5},{7,6},{8,7},{9,8},{10,9},{11,1... | collective-permute-start | bytes 196616 | tf_op jit(solution)/shard_map/ppermute | solution.py:13
  236.1 10.6 %collective-permute-start.22 = (f32[2,1,32,2,128]{4,3,2,0,1:T(2,128)S(1)}, f32[2,1,32,2,128]{4,3,2,0,1:T(2,128)S(1)}, u32[]{:S(2)}, u32[]{:S(2)}) collective-permute-start(f32[2,1,32,2,128]{4,3,2,0,1:T(2,128)S(1)} %get-tuple-element.35), channel_id=1, source_target_pairs={{0,1},{1,2},{2,3},{3,4},{4,5},{5,6},{6,7},{7,8},{8,9},{9,10},{10,1... | collective-permute-start | bytes 196616 | tf_op jit(solution)/shard_map/ppermute | solution.py:13
  240.1 5.9 %collective-permute-start.21 = (f32[1,1,32,2,128]{4,3,2,0,1:T(2,128)S(1)}, f32[1,1,32,2,128]{4,3,2,0,1:T(2,128)S(1)}, u32[]{:S(2)}, u32[]{:S(2)}) collective-permute-start(f32[1,1,32,2,128]{4,3,2,0,1:T(2,128)S(1)} %get-tuple-element.32), channel_id=1, source_target_pairs={{32,0},{64,32},{96,64},{128,96},{160,128},{192,160},{224,192},{33,... | collective-permute-start | bytes 98312 | tf_op jit(solution)/shard_map/ppermute | solution.py:13
  243.4 3.2 collective-permute-start.20
  267.9 13.8 %all-to-all-start.9 = ((f32[8,104,128]{2,1,0:T(8,128)}), f32[8,104,128]{2,1,0:T(8,128)S(1)}, u32[]{:S(2)}, u32[]{:S(2)}) async-start(f32[8,104,128]{2,1,0:T(8,128)} %broadcast_in_dim.72), calls=%async_computation.9 | async-start | bytes 851968 | tf_op jit(solution)/shard_map/all_to_all | solution.py:39
  284.6 11.9 %collective-permute-start.27 = (f32[2,1,32,2,128]{4,3,2,0,1:T(2,128)S(1)}, f32[2,1,32,2,128]{4,3,2,0,1:T(2,128)S(1)}, u32[]{:S(2)}, u32[]{:S(2)}) collective-permute-start(f32[2,1,32,2,128]{4,3,2,0,1:T(2,128)S(1)} %get-tuple-element.30), channel_id=1, source_target_pairs={{1,0},{2,1},{3,2},{4,3},{5,4},{6,5},{7,6},{8,7},{9,8},{10,9},{11,1... | collective-permute-start | bytes 196616 | tf_op jit(solution)/shard_map/ppermute | solution.py:13
  285.9 10.6 %collective-permute-start.26 = (f32[2,1,32,2,128]{4,3,2,0,1:T(2,128)S(1)}, f32[2,1,32,2,128]{4,3,2,0,1:T(2,128)S(1)}, u32[]{:S(2)}, u32[]{:S(2)}) collective-permute-start(f32[2,1,32,2,128]{4,3,2,0,1:T(2,128)S(1)} %get-tuple-element.29), channel_id=1, source_target_pairs={{0,1},{1,2},{2,3},{3,4},{4,5},{5,6},{6,7},{7,8},{8,9},{9,10},{10,1... | collective-permute-start | bytes 196616 | tf_op jit(solution)/shard_map/ppermute | solution.py:13
  289.9 6.2 %collective-permute-start.25 = (f32[1,1,32,2,128]{4,3,2,0,1:T(2,128)S(1)}, f32[1,1,32,2,128]{4,3,2,0,1:T(2,128)S(1)}, u32[]{:S(2)}, u32[]{:S(2)}) collective-permute-start(f32[1,1,32,2,128]{4,3,2,0,1:T(2,128)S(1)} %get-tuple-element.26), channel_id=1, source_target_pairs={{32,0},{64,32},{96,64},{128,96},{160,128},{192,160},{224,192},{33,... | collective-permute-start | bytes 98312 | tf_op jit(solution)/shard_map/ppermute | solution.py:13
  293.2 3.2 collective-permute-start.24
  304.6 13.0 %collective-permute-start.31 = (f32[2,1,32,2,128]{4,3,2,0,1:T(2,128)S(1)}, f32[2,1,32,2,128]{4,3,2,0,1:T(2,128)S(1)}, u32[]{:S(2)}, u32[]{:S(2)}) collective-permute-start(f32[2,1,32,2,128]{4,3,2,0,1:T(2,128)S(1)} %get-tuple-element.24), channel_id=1, source_target_pairs={{1,0},{2,1},{3,2},{4,3},{5,4},{6,5},{7,6},{8,7},{9,8},{10,9},{11,1... | collective-permute-start | bytes 196616 | tf_op jit(solution)/shard_map/ppermute | solution.py:13
  305.9 11.7 %collective-permute-start.30 = (f32[2,1,32,2,128]{4,3,2,0,1:T(2,128)S(1)}, f32[2,1,32,2,128]{4,3,2,0,1:T(2,128)S(1)}, u32[]{:S(2)}, u32[]{:S(2)}) collective-permute-start(f32[2,1,32,2,128]{4,3,2,0,1:T(2,128)S(1)} %get-tuple-element.23), channel_id=1, source_target_pairs={{0,1},{1,2},{2,3},{3,4},{4,5},{5,6},{6,7},{7,8},{8,9},{9,10},{10,1... | collective-permute-start | bytes 196616 | tf_op jit(solution)/shard_map/ppermute | solution.py:13
  309.9 7.2 %collective-permute-start.29 = (f32[1,1,32,2,128]{4,3,2,0,1:T(2,128)S(1)}, f32[1,1,32,2,128]{4,3,2,0,1:T(2,128)S(1)}, u32[]{:S(2)}, u32[]{:S(2)}) collective-permute-start(f32[1,1,32,2,128]{4,3,2,0,1:T(2,128)S(1)} %get-tuple-element.20), channel_id=1, source_target_pairs={{32,0},{64,32},{96,64},{128,96},{160,128},{192,160},{224,192},{33,... | collective-permute-start | bytes 98312 | tf_op jit(solution)/shard_map/ppermute | solution.py:13
  312.4 5.2 %collective-permute-start.28 = (f32[1,1,32,2,128]{4,3,2,0,1:T(2,128)S(1)}, f32[1,1,32,2,128]{4,3,2,0,1:T(2,128)S(1)}, u32[]{:S(2)}, u32[]{:S(2)}) collective-permute-start(f32[1,1,32,2,128]{4,3,2,0,1:T(2,128)S(1)} %get-tuple-element.19), channel_id=1, source_target_pairs={{0,32},{32,64},{64,96},{96,128},{128,160},{160,192},{192,224},{1,3... | collective-permute-start | bytes 98312 | tf_op jit(solution)/shard_map/ppermute | solution.py:13
  343.6 13.9 %all-to-all-start.11 = ((f32[8,112,128]{2,1,0:T(8,128)}), f32[8,112,128]{2,1,0:T(8,128)S(1)}, u32[]{:S(2)}, u32[]{:S(2)}) async-start(f32[8,112,128]{2,1,0:T(8,128)} %broadcast_in_dim.76), calls=%async_computation.11 | async-start | bytes 917504 | tf_op jit(solution)/shard_map/all_to_all | solution.py:39
  366.8 12.0 %collective-permute-start.35 = (f32[2,1,32,2,128]{4,3,2,0,1:T(2,128)S(1)}, f32[2,1,32,2,128]{4,3,2,0,1:T(2,128)S(1)}, u32[]{:S(2)}, u32[]{:S(2)}) collective-permute-start(f32[2,1,32,2,128]{4,3,2,0,1:T(2,128)S(1)} %get-tuple-element.18), channel_id=1, source_target_pairs={{1,0},{2,1},{3,2},{4,3},{5,4},{6,5},{7,6},{8,7},{9,8},{10,9},{11,1... | collective-permute-start | bytes 196616 | tf_op jit(solution)/shard_map/ppermute | solution.py:13
  368.1 10.7 %collective-permute-start.34 = (f32[2,1,32,2,128]{4,3,2,0,1:T(2,128)S(1)}, f32[2,1,32,2,128]{4,3,2,0,1:T(2,128)S(1)}, u32[]{:S(2)}, u32[]{:S(2)}) collective-permute-start(f32[2,1,32,2,128]{4,3,2,0,1:T(2,128)S(1)} %get-tuple-element.17), channel_id=1, source_target_pairs={{0,1},{1,2},{2,3},{3,4},{4,5},{5,6},{6,7},{7,8},{8,9},{9,10},{10,1... | collective-permute-start | bytes 196616 | tf_op jit(solution)/shard_map/ppermute | solution.py:13
  372.1 6.7 %collective-permute-start.33 = (f32[1,1,32,2,128]{4,3,2,0,1:T(2,128)S(1)}, f32[1,1,32,2,128]{4,3,2,0,1:T(2,128)S(1)}, u32[]{:S(2)}, u32[]{:S(2)}) collective-permute-start(f32[1,1,32,2,128]{4,3,2,0,1:T(2,128)S(1)} %get-tuple-element.14), channel_id=1, source_target_pairs={{32,0},{64,32},{96,64},{128,96},{160,128},{192,160},{224,192},{33,... | collective-permute-start | bytes 98312 | tf_op jit(solution)/shard_map/ppermute | solution.py:13
  375.5 3.4 collective-permute-start.32
